TPU v7x, 256 devices: a whole 4x4x8 slice. The times are simulated.
256 devices in a mesh: lev: 8 (over x_lo, y), tile: 32 (over x_hi, z, core).
Axes of the slice: x: 4 (x_hi: 2, x_lo: 2; x = x_hi * 2 + x_lo), y: 4, z: 8, core: 2. Of those that a mesh axis runs over, the one named last changes fastest.
Arguments:
- cotangent: bfloat16 [72, 96, 32768], P('lev', None, 'tile'), may hold values from -6 to 6
- particles: bfloat16 [72, 96, 32768], P('lev', None, 'tile'), may hold values from 0.049804688 to 2
- coag_rate: float32 [72], P('lev'), may hold values from 0.004 to 0.015
- courant: float32 [2, 72, 32768], P(None, 'lev', 'tile'), may hold values from 0.05 to 0.45
- offsets: int32 [2, 32768], P(None, 'tile'), may hold values from -2 to 2
- mass_flux: bfloat16 [72, 72, 32768], P(None, None, ('tile', 'lev')), may hold values from -0.75 to 0.75
- cloud_top: int32 [32768], P(('tile', 'lev')), may hold values from 18 to 71
Outputs:
- result: float32 [72, 96, 32768], P(None, None, ('tile', 'lev'))
All inputs are finite; a program needn't handle non-finite values.
Results may differ from a plain program's by a relative error of at most 0.0029.
Values may be sent and summed in bfloat16 or wider, within the bound.
No kernel may reach another device: no remote copies, remote signals or barrier semaphores. Data moves between devices by JAX's collectives and lax.ppermute only.
A program may use at most 64 MiB of HBM per device.

v0:
```python
import math
import jax
import jax.numpy as jnp
from jax import lax
from jax.sharding import PartitionSpec as P

NX = 128
REACH = 2


def extended(cells, sides, width):
    for axis, dim in sides:
        count = lax.axis_size(axis)
        ends = count - 1
        head = lax.slice_in_dim(cells, 0, width, axis=dim)
        tail = lax.slice_in_dim(cells, cells.shape[dim] - width, cells.shape[dim], axis=dim)
        cells = jnp.concatenate(
            [
                lax.ppermute(tail, axis, [(i, (i + 1) % count) for i in range(ends)]),
                cells,
                lax.ppermute(head, axis, [((i + 1) % count, i) for i in range(ends)]),
            ],
            axis=dim,
        )
    return cells


def make_tables(bins, freq_count):
    length = 2 * bins
    bin_index = lax.broadcasted_iota(jnp.int32, (freq_count, bins), 1)
    freq_index = lax.broadcasted_iota(jnp.int32, (freq_count, bins), 0)
    phase_angle = (bin_index * freq_index % length).astype(jnp.float32) * (2.0 * math.pi / length)
    kept_freq = freq_index >= 0
    weight = jnp.ones((freq_count, bins), jnp.float32)
    forward_table = jnp.concatenate(
        [
            jnp.where(kept_freq, jnp.cos(phase_angle), 0.0),
            jnp.where(kept_freq, -jnp.sin(phase_angle), 0.0),
        ],
        axis=0,
    ).astype(jnp.bfloat16)
    inverse_cos = (jnp.transpose(weight * jnp.cos(phase_angle)) / length).astype(jnp.bfloat16)
    inverse_sin = (jnp.transpose(-weight * jnp.sin(phase_angle)) / length).astype(jnp.bfloat16)
    return (forward_table, inverse_cos, inverse_sin)


def coagulate(gradients, amounts, coag_rate, tables, freq_count):
    forward_table, inverse_cos, inverse_sin = tables

    def one_level(pieces):
        gradient, particles, coefficient = pieces
        grad_spec = jnp.dot(forward_table, gradient, preferred_element_type=jnp.float32)
        mass_spec = jnp.dot(forward_table, particles, preferred_element_type=jnp.float32)
        grad_re = grad_spec[:freq_count]
        grad_im = grad_spec[freq_count:]
        mass_re = mass_spec[:freq_count]
        mass_im = mass_spec[freq_count:]
        prod_re = (mass_re * grad_re + mass_im * grad_im).astype(jnp.bfloat16)
        prod_im = (mass_re * grad_im - mass_im * grad_re).astype(jnp.bfloat16)
        correlation = jnp.dot(inverse_cos, prod_re, preferred_element_type=jnp.float32) + jnp.dot(
            inverse_sin, prod_im, preferred_element_type=jnp.float32
        )
        grad_wide = gradient.astype(jnp.float32)
        mass_wide = particles.astype(jnp.float32)
        total_mass = jnp.sum(mass_wide, axis=0)
        inner = jnp.sum(grad_wide * mass_wide, axis=0)
        return grad_wide + coefficient * (correlation - grad_wide * total_mass - inner)

    return lax.map(one_level, (gradients, amounts, coag_rate))


def body(cotangent, particles, coag_rate, courant, offsets, mass_flux, cloud_top):
    level_count, bins, cell_count = cotangent.shape
    row_count = cell_count // NX
    freq_count = 2 * bins
    tables = make_tables(bins, freq_count)
    adjoint = coagulate(cotangent, particles, coag_rate, tables, freq_count)
    adjoint = extended(adjoint.reshape(level_count, bins, row_count, NX), (("tile", 2),), REACH)
    centre_rows = adjoint[:, :, REACH : REACH + row_count, :]
    cour_y = courant[0].reshape(level_count, 1, row_count, NX)
    cour_x = courant[1].reshape(level_count, 1, row_count, NX)
    shift_y = offsets[0].reshape(row_count, NX)
    shift_x = offsets[1].reshape(row_count, NX)
    pad_x = jnp.pad(centre_rows, ((0, 0), (0, 0), (0, 0), (REACH, REACH)))
    along_y = jnp.zeros_like(centre_rows)
    along_x = jnp.zeros_like(centre_rows)
    for upwind in range(-REACH, REACH + 1):
        along_y = along_y + jnp.where(
            shift_y == upwind, adjoint[:, :, REACH + upwind : REACH + upwind + row_count, :], 0.0
        )
        along_x = along_x + jnp.where(
            shift_x == upwind, pad_x[:, :, :, REACH + upwind : REACH + upwind + NX], 0.0
        )
    remapped = centre_rows * (1.0 - cour_y - cour_x) + cour_y * along_y + cour_x * along_x
    remapped = remapped.astype(jnp.bfloat16).reshape(level_count, bins, cell_count)
    all_levels = mass_flux.shape[0]
    level_ids = lax.broadcasted_iota(jnp.int32, (all_levels, cloud_top.shape[0]), 0)
    inside = level_ids <= cloud_top[None, :]
    masked = jnp.where(
        inside[:, None, :] & inside[None, :, :], mass_flux, jnp.zeros_like(mass_flux)
    )
    received = lax.all_to_all(remapped, "lev", split_axis=2, concat_axis=0, tiled=True)
    mixing = jnp.einsum("obc,oic->ibc", received, masked, preferred_element_type=jnp.float32)
    return received.astype(jnp.float32) + mixing


def solution(mesh):
    placed = (
        P("lev", None, "tile"),
        P("lev", None, "tile"),
        P("lev"),
        P(None, "lev", "tile"),
        P(None, "tile"),
        P(None, None, ("tile", "lev")),
        P(("tile", "lev")),
    )
    return jax.shard_map(
        body, mesh=mesh, in_specs=placed, out_specs=P(None, None, ("tile", "lev")), check_vma=False
    )
```

profile of v0, /device:TPU:6, one launch (start us, length us, event | category | flops | bytes accessed | tf_op | source)
XLA Modules:
  0.0 171.8 jit_solution(14030658634548506464)
XLA Ops:
  0.5 72.2 %while.11 = (s32[]{:T(128)}, f32[9,96,1024]{2,1,0:T(8,128)}, bf16[9,96,1024]{2,1,0:T(8,128)(2,1)}, f32[9]{0:T(128)}, bf16[9,96,1024]{2,1,0:T(8,128)(2,1)}, /*index=5*/bf16[384,96]{1,0:T(8,128)(2,1)S(1)}, s32[]{:T(128)}) while((s32[]{:T(128)}, f32[9,96,1024]{2,1,0:T(8,128)}, bf16[9,96,1024]{2,1,0:T(8,128)(2,1)}, f32[9]{0:T(128)}, ...), condition=%wide.region_3.4_spmd.clone, body=%wide.region_0.3_spmd.clone.sunk | while | flops 229648384 | bytes 11766025 | solution.py:69
  0.5 1.3 convolution_bitcast_fusion.4
  1.8 1.3 convolution_bitcast_fusion.5
  3.7 1.1 convert_reduce_fusion.2
  5.5 3.0 %fusion.83 = f32[9,96,1024]{2,1,0:T(8,128)} fusion(f32[9,96,1024]{2,1,0:T(8,128)} %get-tuple-element.142, s32[]{:T(128)} %get-tuple-element.141, f32[1024,96]{0,1:T(8,128)S(1)} %fusion.82, f32[384,1024]{1,0:T(8,128)S(1)} %convolution_bitcast_fusion.4, f32[384,1024]{1,0:T(8,128)S(1)} %convolution_bitcast_fusion.5, f32[1024]{0:T(1024)S(1)} %get-tuple-element.132, ...), kind=kOutput, calls=%fused_computation.11.clone.1 | convolution fusion | flops 39426048 | bytes 4137984 | tf_op jit(solution)/shard_map/while/body/eval_jaxpr/dot_general | solution.py:60
  8.5 1.3 convolution_bitcast_fusion.4
  9.8 1.3 convolution_bitcast_fusion.5
  11.7 1.1 convert_reduce_fusion.2
  13.5 3.0 %fusion.83 = f32[9,96,1024]{2,1,0:T(8,128)} fusion(f32[9,96,1024]{2,1,0:T(8,128)} %get-tuple-element.142, s32[]{:T(128)} %get-tuple-element.141, f32[1024,96]{0,1:T(8,128)S(1)} %fusion.82, f32[384,1024]{1,0:T(8,128)S(1)} %convolution_bitcast_fusion.4, f32[384,1024]{1,0:T(8,128)S(1)} %convolution_bitcast_fusion.5, f32[1024]{0:T(1024)S(1)} %get-tuple-element.132, ...), kind=kOutput, calls=%fused_computation.11.clone.1 | convolution fusion | flops 39426048 | bytes 4137984 | tf_op jit(solution)/shard_map/while/body/eval_jaxpr/dot_general | solution.py:60
  16.5 1.3 convolution_bitcast_fusion.4
  17.8 1.3 convolution_bitcast_fusion.5
  21.5 3.0 %fusion.83 = f32[9,96,1024]{2,1,0:T(8,128)} fusion(f32[9,96,1024]{2,1,0:T(8,128)} %get-tuple-element.142, s32[]{:T(128)} %get-tuple-element.141, f32[1024,96]{0,1:T(8,128)S(1)} %fusion.82, f32[384,1024]{1,0:T(8,128)S(1)} %convolution_bitcast_fusion.4, f32[384,1024]{1,0:T(8,128)S(1)} %convolution_bitcast_fusion.5, f32[1024]{0:T(1024)S(1)} %get-tuple-element.132, ...), kind=kOutput, calls=%fused_computation.11.clone.1 | convolution fusion | flops 39426048 | bytes 4137984 | tf_op jit(solution)/shard_map/while/body/eval_jaxpr/dot_general | solution.py:60
  24.6 1.3 convolution_bitcast_fusion.4
  25.9 1.3 convolution_bitcast_fusion.5
  29.6 3.0 %fusion.83 = f32[9,96,1024]{2,1,0:T(8,128)} fusion(f32[9,96,1024]{2,1,0:T(8,128)} %get-tuple-element.142, s32[]{:T(128)} %get-tuple-element.141, f32[1024,96]{0,1:T(8,128)S(1)} %fusion.82, f32[384,1024]{1,0:T(8,128)S(1)} %convolution_bitcast_fusion.4, f32[384,1024]{1,0:T(8,128)S(1)} %convolution_bitcast_fusion.5, f32[1024]{0:T(1024)S(1)} %get-tuple-element.132, ...), kind=kOutput, calls=%fused_computation.11.clone.1 | convolution fusion | flops 39426048 | bytes 4137984 | tf_op jit(solution)/shard_map/while/body/eval_jaxpr/dot_general | solution.py:60
  32.6 1.3 convolution_bitcast_fusion.4
  33.9 1.3 convolution_bitcast_fusion.5
  37.6 3.0 %fusion.83 = f32[9,96,1024]{2,1,0:T(8,128)} fusion(f32[9,96,1024]{2,1,0:T(8,128)} %get-tuple-element.142, s32[]{:T(128)} %get-tuple-element.141, f32[1024,96]{0,1:T(8,128)S(1)} %fusion.82, f32[384,1024]{1,0:T(8,128)S(1)} %convolution_bitcast_fusion.4, f32[384,1024]{1,0:T(8,128)S(1)} %convolution_bitcast_fusion.5, f32[1024]{0:T(1024)S(1)} %get-tuple-element.132, ...), kind=kOutput, calls=%fused_computation.11.clone.1 | convolution fusion | flops 39426048 | bytes 4137984 | tf_op jit(solution)/shard_map/while/body/eval_jaxpr/dot_general | solution.py:60
  40.6 1.3 convolution_bitcast_fusion.4
  41.9 1.3 convolution_bitcast_fusion.5
  45.6 3.0 %fusion.83 = f32[9,96,1024]{2,1,0:T(8,128)} fusion(f32[9,96,1024]{2,1,0:T(8,128)} %get-tuple-element.142, s32[]{:T(128)} %get-tuple-element.141, f32[1024,96]{0,1:T(8,128)S(1)} %fusion.82, f32[384,1024]{1,0:T(8,128)S(1)} %convolution_bitcast_fusion.4, f32[384,1024]{1,0:T(8,128)S(1)} %convolution_bitcast_fusion.5, f32[1024]{0:T(1024)S(1)} %get-tuple-element.132, ...), kind=kOutput, calls=%fused_computation.11.clone.1 | convolution fusion | flops 39426048 | bytes 4137984 | tf_op jit(solution)/shard_map/while/body/eval_jaxpr/dot_general | solution.py:60
  48.6 1.3 convolution_bitcast_fusion.4
  49.9 1.3 convolution_bitcast_fusion.5
  53.6 3.0 %fusion.83 = f32[9,96,1024]{2,1,0:T(8,128)} fusion(f32[9,96,1024]{2,1,0:T(8,128)} %get-tuple-element.142, s32[]{:T(128)} %get-tuple-element.141, f32[1024,96]{0,1:T(8,128)S(1)} %fusion.82, f32[384,1024]{1,0:T(8,128)S(1)} %convolution_bitcast_fusion.4, f32[384,1024]{1,0:T(8,128)S(1)} %convolution_bitcast_fusion.5, f32[1024]{0:T(1024)S(1)} %get-tuple-element.132, ...), kind=kOutput, calls=%fused_computation.11.clone.1 | convolution fusion | flops 39426048 | bytes 4137984 | tf_op jit(solution)/shard_map/while/body/eval_jaxpr/dot_general | solution.py:60
  56.7 1.3 convolution_bitcast_fusion.4
  58.0 1.3 convolution_bitcast_fusion.5
  61.7 3.0 %fusion.83 = f32[9,96,1024]{2,1,0:T(8,128)} fusion(f32[9,96,1024]{2,1,0:T(8,128)} %get-tuple-element.142, s32[]{:T(128)} %get-tuple-element.141, f32[1024,96]{0,1:T(8,128)S(1)} %fusion.82, f32[384,1024]{1,0:T(8,128)S(1)} %convolution_bitcast_fusion.4, f32[384,1024]{1,0:T(8,128)S(1)} %convolution_bitcast_fusion.5, f32[1024]{0:T(1024)S(1)} %get-tuple-element.132, ...), kind=kOutput, calls=%fused_computation.11.clone.1 | convolution fusion | flops 39426048 | bytes 4137984 | tf_op jit(solution)/shard_map/while/body/eval_jaxpr/dot_general | solution.py:60
  64.7 1.3 convolution_bitcast_fusion.4
  66.0 1.3 convolution_bitcast_fusion.5
  69.7 3.0 %fusion.83 = f32[9,96,1024]{2,1,0:T(8,128)} fusion(f32[9,96,1024]{2,1,0:T(8,128)} %get-tuple-element.142, s32[]{:T(128)} %get-tuple-element.141, f32[1024,96]{0,1:T(8,128)S(1)} %fusion.82, f32[384,1024]{1,0:T(8,128)S(1)} %convolution_bitcast_fusion.4, f32[384,1024]{1,0:T(8,128)S(1)} %convolution_bitcast_fusion.5, f32[1024]{0:T(1024)S(1)} %get-tuple-element.132, ...), kind=kOutput, calls=%fused_computation.11.clone.1 | convolution fusion | flops 39426048 | bytes 4137984 | tf_op jit(solution)/shard_map/while/body/eval_jaxpr/dot_general | solution.py:60
  72.7 2.8 %copy.77 = f32[108,8,8,128]{3,2,1,0:T(8,128)S(1)} copy(f32[108,8,8,128]{3,1,2,0:T(8,128)} %bitcast.27) | data formatting | bytes 7077888
  76.3 1.9 %collective-permute-start = (f32[9,96,2,128]{3,1,2,0:T(8,128)S(1)}, f32[9,96,2,128]{3,1,2,0:T(8,128)S(1)}, u32[]{:S(2)}, u32[]{:S(2)}) collective-permute-start(f32[9,96,2,128]{3,1,2,0:T(8,128)S(1)} %copy.64), channel_id=1, source_target_pairs={{0,1},{1,2},{2,3},{3,4},{4,5},{5,6},{6,7},{7,8},{8,9},{9,10},{10,1... | collective-permute-start | bytes 2654216 | tf_op jit(solution)/shard_map/ppermute | solution.py:19
  78.4 8.1 %collective-permute-start.1 = (f32[9,96,2,128]{3,1,2,0:T(8,128)S(1)}, f32[9,96,2,128]{3,1,2,0:T(8,128)S(1)}, u32[]{:S(2)}, u32[]{:S(2)}) collective-permute-start(f32[9,96,2,128]{3,1,2,0:T(8,128)S(1)} %copy.66), channel_id=1, source_target_pairs={{1,0},{2,1},{3,2},{4,3},{5,4},{6,5},{7,6},{8,7},{9,8},{10,9},{11,1... | collective-permute-start | bytes 2654216 | tf_op jit(solution)/shard_map/ppermute | solution.py:21
  87.5 7.6 %collective-permute-done = f32[9,96,2,128]{3,1,2,0:T(8,128)S(1)} collective-permute-done((f32[9,96,2,128]{3,1,2,0:T(8,128)S(1)}, f32[9,96,2,128]{3,1,2,0:T(8,128)S(1)}, u32[]{:S(2)}, u32[]{:S(2)}) %collective-permute-start) | collective-permute-done | bytes 884768 | tf_op jit(solution)/shard_map/ppermute | solution.py:19
  95.8 1.2 collective-permute-done.1
  98.0 6.1 %fusion.49 = bf16[9,96,8,128]{3,2,1,0:T(8,128)(2,1)S(1)} fusion(f32[9,96,2,128]{3,2,1,0:T(2,128)S(1)} %copy.65, f32[9,96,8,128]{3,2,1,0:T(8,128)S(1)} %bitcast.90, f32[9,96,10,128]{3,2,1,0:T(8,128)S(1)} %copy_dynamic-update-slice_fusion, f32[9,8,128]{2,1,0:T(8,128)S(1)} %bitcast.97, f32[9,8,128]{2,1,0:T(8,128)S(1)} %bitcast.95, ...), kind=kLoop, calls=%fused_computation.63 | loop fusion | flops 23003136 | bytes 13391872 | tf_op jit(solution)/shard_map/convert_element_type | solution.py:95
  104.1 4.7 %copy.74 = bf16[9,96,8,128]{1,0,3,2:T(8,128)(2,1)} copy(bf16[9,96,8,128]{3,2,1,0:T(8,128)(2,1)S(1)} %fusion.49) | data formatting | bytes 3538944 | tf_op jit(solution)/shard_map/reshape | solution.py:95
  108.8 8.0 %reshape.88 = bf16[8,2,55296]{2,1,0:T(2,128)(2,1)} reshape(bf16[1024,9,96]{2,1,0:T(8,128)(2,1)} %bitcast.91) | data formatting | bytes 3538944
  116.8 5.9 %all-to-all-start = ((bf16[8,2,55296]{2,1,0:T(2,128)(2,1)}), bf16[8,2,55296]{2,1,0:T(2,128)(2,1)S(1)}, u32[]{:S(2)}, u32[]{:S(2)}) async-start(bf16[8,2,55296]{2,1,0:T(2,128)(2,1)} %reshape.88), calls=%async_computation | async-start | bytes 3538944 | tf_op jit(solution)/shard_map/all_to_all | solution.py:102
  122.7 1.8 %and_select_fusion = bf16[72,72,128]{2,1,0:T(8,128)(2,1)S(1)} fusion(bf16[72,72,128]{2,1,0:T(8,128)(2,1)} %param.14, pred[72,128]{1,0:T(8,128)(4,1)S(1)} %iota_compare_fusion), kind=kLoop, calls=%fused_computation.78 | loop fusion | flops 1327104 | bytes 2663424 | tf_op jit(solution)/shard_map/jit(_where)/select_n | solution.py:99
  124.5 2.7 %copy.71 = bf16[72,72,128]{0,1,2:T(8,128)(2,1)} copy(bf16[72,72,128]{2,1,0:T(8,128)(2,1)S(1)} %and_select_fusion) | data formatting | bytes 2654208 | tf_op jit(solution)/shard_map/jit(_where)/select_n | solution.py:99
  127.3 15.6 %all-to-all-done = bf16[8,2,55296]{2,1,0:T(2,128)(2,1)S(1)} async-done(((bf16[8,2,55296]{2,1,0:T(2,128)(2,1)}), bf16[8,2,55296]{2,1,0:T(2,128)(2,1)S(1)}, u32[]{:S(2)}, u32[]{:S(2)}) %all-to-all-start) | async-done | bytes 1769504 | tf_op jit(solution)/shard_map/all_to_all | solution.py:102
  142.9 6.2 %reshape.89 = bf16[1024,9,96]{2,1,0:T(8,128)(2,1)} reshape(bf16[8,2,55296]{2,1,0:T(2,128)(2,1)S(1)} %all-to-all-done) | data formatting | bytes 3538944
  149.1 4.1 %copy.70 = bf16[8,9,96,128]{3,2,1,0:T(8,128)(2,1)S(1)} copy(bf16[8,9,96,128]{2,1,3,0:T(8,128)(2,1)} %bitcast.92) | data formatting | bytes 3538944 | tf_op jit(solution)/shard_map/all_to_all | solution.py:102
  153.2 2.7 %copy.72 = bf16[72,96,128]{1,0,2:T(8,128)(2,1)} copy(bf16[72,96,128]{2,1,0:T(8,128)(2,1)S(1)} %bitcast.93) | data formatting | bytes 3538944 | tf_op jit(solution)/shard_map/all_to_all | solution.py:102
  156.0 5.9 %fusion.67 = f32[128,72,96]{2,1,0:T(8,128)} fusion(bf16[72,72,128]{0,1,2:T(8,128)(2,1)} %copy.71, bf16[72,96,128]{1,0,2:T(8,128)(2,1)} %copy.72), kind=kOutput, calls=%fused_computation.105 | convolution fusion | flops 127401984 | bytes 6635520 | tf_op jit(solution)/shard_map/obc,oic->ibc/dot_general | solution.py:103
  161.9 5.7 %copy.73 = f32[128,72,96]{0,2,1:T(8,128)} copy(f32[128,72,96]{2,1,0:T(8,128)} %fusion.67) | data formatting | bytes 7077888 | tf_op jit(solution)/shard_map/obc,oic->ibc/dot_general | solution.py:103
  167.5 4.3 %bitcast_add_fusion = f32[72,96,128]{2,1,0:T(8,128)} fusion(f32[128,72,96]{0,2,1:T(8,128)} %copy.73, bf16[8,9,96,128]{3,2,1,0:T(8,128)(2,1)S(1)} %copy.70), kind=kLoop, calls=%fused_computation.77 | loop fusion | flops 1769472 | bytes 8847360 | tf_op jit(solution)/shard_map/add | solution.py:104
  (62 shorter events, 23.6 us)
Async XLA Ops:
  0.5 4.3 %copy-start.3 = (f32[9]{0:T(128)S(1)}, f32[9]{0:T(128)}, u32[]{:S(2)}) copy-start(f32[9]{0:T(128)} %get-tuple-element.151) | copy-start | bytes 112 | tf_op jit(solution)/shard_map/while
  8.5 4.3 %copy-start.3 = (f32[9]{0:T(128)S(1)}, f32[9]{0:T(128)}, u32[]{:S(2)}) copy-start(f32[9]{0:T(128)} %get-tuple-element.151) | copy-start | bytes 112 | tf_op jit(solution)/shard_map/while
  16.5 4.3 %copy-start.3 = (f32[9]{0:T(128)S(1)}, f32[9]{0:T(128)}, u32[]{:S(2)}) copy-start(f32[9]{0:T(128)} %get-tuple-element.151) | copy-start | bytes 112 | tf_op jit(solution)/shard_map/while
  24.6 4.3 %copy-start.3 = (f32[9]{0:T(128)S(1)}, f32[9]{0:T(128)}, u32[]{:S(2)}) copy-start(f32[9]{0:T(128)} %get-tuple-element.151) | copy-start | bytes 112 | tf_op jit(solution)/shard_map/while
  32.6 4.3 %copy-start.3 = (f32[9]{0:T(128)S(1)}, f32[9]{0:T(128)}, u32[]{:S(2)}) copy-start(f32[9]{0:T(128)} %get-tuple-element.151) | copy-start | bytes 112 | tf_op jit(solution)/shard_map/while
  40.6 4.3 %copy-start.3 = (f32[9]{0:T(128)S(1)}, f32[9]{0:T(128)}, u32[]{:S(2)}) copy-start(f32[9]{0:T(128)} %get-tuple-element.151) | copy-start | bytes 112 | tf_op jit(solution)/shard_map/while
  48.6 4.3 %copy-start.3 = (f32[9]{0:T(128)S(1)}, f32[9]{0:T(128)}, u32[]{:S(2)}) copy-start(f32[9]{0:T(128)} %get-tuple-element.151) | copy-start | bytes 112 | tf_op jit(solution)/shard_map/while
  56.7 4.3 %copy-start.3 = (f32[9]{0:T(128)S(1)}, f32[9]{0:T(128)}, u32[]{:S(2)}) copy-start(f32[9]{0:T(128)} %get-tuple-element.151) | copy-start | bytes 112 | tf_op jit(solution)/shard_map/while
  64.7 4.3 %copy-start.3 = (f32[9]{0:T(128)S(1)}, f32[9]{0:T(128)}, u32[]{:S(2)}) copy-start(f32[9]{0:T(128)} %get-tuple-element.151) | copy-start | bytes 112 | tf_op jit(solution)/shard_map/while
  75.6 10.9 %copy-start.1 = (s32[2,1024]{1,0:T(2,128)S(1)}, s32[2,1024]{1,0:T(2,128)}, u32[]{:S(2)}) copy-start(s32[2,1024]{1,0:T(2,128)} %param.13) | copy-start | bytes 24580
  76.3 18.8 %collective-permute-start = (f32[9,96,2,128]{3,1,2,0:T(8,128)S(1)}, f32[9,96,2,128]{3,1,2,0:T(8,128)S(1)}, u32[]{:S(2)}, u32[]{:S(2)}) collective-permute-start(f32[9,96,2,128]{3,1,2,0:T(8,128)S(1)} %copy.64), channel_id=1, source_target_pairs={{0,1},{1,2},{2,3},{3,4},{4,5},{5,6},{6,7},{7,8},{8,9},{9,10},{10,1... | collective-permute-start | bytes 2654216 | tf_op jit(solution)/shard_map/ppermute | solution.py:19
  78.4 18.6 %collective-permute-start.1 = (f32[9,96,2,128]{3,1,2,0:T(8,128)S(1)}, f32[9,96,2,128]{3,1,2,0:T(8,128)S(1)}, u32[]{:S(2)}, u32[]{:S(2)}) collective-permute-start(f32[9,96,2,128]{3,1,2,0:T(8,128)S(1)} %copy.66), channel_id=1, source_target_pairs={{1,0},{2,1},{3,2},{4,3},{5,4},{6,5},{7,6},{8,7},{9,8},{10,9},{11,1... | collective-permute-start | bytes 2654216 | tf_op jit(solution)/shard_map/ppermute | solution.py:21
  86.6 0.9 copy-start
  108.8 14.0 %copy-start.2 = (s32[128]{0:T(128)S(1)}, s32[128]{0:T(128)}, u32[]{:S(2)}) copy-start(s32[128]{0:T(128)} %param.15) | copy-start | bytes 1540
  116.8 26.1 %all-to-all-start = ((bf16[8,2,55296]{2,1,0:T(2,128)(2,1)}), bf16[8,2,55296]{2,1,0:T(2,128)(2,1)S(1)}, u32[]{:S(2)}, u32[]{:S(2)}) async-start(bf16[8,2,55296]{2,1,0:T(2,128)(2,1)} %reshape.88), calls=%async_computation | async-start | bytes 3538944 | tf_op jit(solution)/shard_map/all_to_all | solution.py:102
where the time goes:
time: 173 us; the launch traced here: 172 us
  matrix products  61.8 us (36%)
  local copies, waits for them, and re-layouts  46.5 us (27%)
  waiting for transfers between devices  24.4 us (14%)
  other arithmetic  22.9 us (13%)
  starting transfers between devices  15.9 us (9%)
    dot_general x9, matrix products, one_level(): jnp.dot(inverse_sin, prod_im, preferred_element_type=jnp.float32)  27.2 us
    unnamed x10, local copies, waits for them, and re-layouts  17.9 us
    all_to_all x1, waiting for transfers between devices, body(): lax.all_to_all(remapped, 'lev', split_axis=2, concat_axis=0, tiled=True)  15.6 us
    dot_general x9, matrix products, one_level(): jnp.dot(forward_table, gradient, preferred_element_type=jnp.float32)  11.6 us
    dot_general x9, matrix products, one_level(): jnp.dot(forward_table, particles, preferred_element_type=jnp.float32)  11.5 us
    reduce_sum x9, other arithmetic, one_level(): total_mass = jnp.sum(mass_wide, axis=0)  10 us
    ppermute x1, starting transfers between devices, extended(): lax.ppermute(head, axis, [((i + 1) % count, i) for i in range(ends)])  8.05 us
    ppermute x1, waiting for transfers between devices, extended(): lax.ppermute(tail, axis, [(i, (i + 1) % count) for i in range(ends)])  7.59 us
  transfers between devices with their start and end apart: 3, of which 3 were waited for; matrix products, arithmetic and copies ran while one was open for 3% of the time, Pallas kernels for 0%

commit v1 on v0

--- a/solution.py
+++ b/solution.py
@@ -99,7 +99,8 @@
     masked = jnp.where(
         inside[:, None, :] & inside[None, :, :], mass_flux, jnp.zeros_like(mass_flux)
     )
-    received = lax.all_to_all(remapped, "lev", split_axis=2, concat_axis=0, tiled=True)
+    z = lax.all_to_all(jnp.stack(jnp.split(remapped, lax.axis_size("lev"), axis=2)), "lev", 0, 0)
+    received = jnp.concatenate(z, axis=0)
     mixing = jnp.einsum("obc,oic->ibc", received, masked, preferred_element_type=jnp.float32)
     return received.astype(jnp.float32) + mixing
 

time: 173 us -> 155 us (0.90)
  local copies, waits for them, and re-layouts: 46.5 us -> 28.8 us
    unnamed x10 -> x15, local copies, waits for them, and re-layouts: 17.9 us -> 8.91 us
    all_to_all x2 -> x0, local copies, waits for them, and re-layouts: 6.87 us -> none  [body(): lax.all_to_all(remapped, 'lev', split_axis=2, concat_axis=0, tiled=True)]
    ppermute x1, waiting for transfers between devices: 1.16 us -> 7.51 us  [extended(): lax.ppermute(head, axis, [((i + 1) % count, i) for i in range(ends)])]
    all_to_all x1, waiting for transfers between devices: 15.6 us -> 9.34 us  [body(): lax.all_to_all(jnp.stack(jnp.split(remapped, lax.axis_size('lev'), axis=2...]
    reshape x1, local copies, waits for them, and re-layouts: 4.68 us -> 0.81 us  [body(): remapped.astype(jnp.bfloat16).reshape(level_count, bins, cell_count)]
    reshape x0 -> x1, local copies, waits for them, and re-layouts: none -> 2.74 us  [body(): received = jnp.concatenate(z, axis=0)]
  transfers between devices with their start and end apart: 3 -> 3, of which waited for: 3 -> 3; matrix products, arithmetic and copies ran while one was open for 3% -> 4% of each run, Pallas kernels for 0% -> 0%
where the time goes in v1:
time: 155 us; the launch traced here: 154 us
  matrix products  61.6 us (40%)
  local copies, waits for them, and re-layouts  28.8 us (19%)
  waiting for transfers between devices  23.9 us (15%)
  other arithmetic  22.8 us (15%)
  starting transfers between devices  15.9 us (10%)
    dot_general x9, matrix products, one_level(): jnp.dot(inverse_sin, prod_im, preferred_element_type=jnp.float32)  27.2 us
    dot_general x9, matrix products, one_level(): jnp.dot(forward_table, particles, preferred_element_type=jnp.float32)  11.5 us
    dot_general x9, matrix products, one_level(): jnp.dot(forward_table, gradient, preferred_element_type=jnp.float32)  11.4 us
    reduce_sum x9, other arithmetic, one_level(): total_mass = jnp.sum(mass_wide, axis=0)  10 us
    all_to_all x1, waiting for transfers between devices, body(): lax.all_to_all(jnp.stack(jnp.split(remapped, lax.axis_size('lev'), axis=2...  9.34 us
    unnamed x15, local copies, waits for them, and re-layouts  8.91 us
    ppermute x1, starting transfers between devices, extended(): lax.ppermute(head, axis, [((i + 1) % count, i) for i in range(ends)])  8.05 us
    ppermute x1, waiting for transfers between devices, extended(): lax.ppermute(head, axis, [((i + 1) % count, i) for i in range(ends)])  7.51 us
  transfers between devices with their start and end apart: 3, of which 3 were waited for; matrix products, arithmetic and copies ran while one was open for 4% of the time, Pallas kernels for 0%

profile of v1, /device:TPU:6, one launch (start us, length us, event | category | flops | bytes accessed | tf_op | source)
XLA Modules:
  0.0 153.5 jit_solution(11630961382888933139)
XLA Ops:
  0.5 72.2 %while.11 = (s32[]{:T(128)}, f32[9,96,1024]{2,1,0:T(8,128)}, bf16[9,96,1024]{2,1,0:T(8,128)(2,1)}, f32[9]{0:T(128)}, bf16[9,96,1024]{2,1,0:T(8,128)(2,1)}, /*index=5*/bf16[384,96]{1,0:T(8,128)(2,1)S(1)}, s32[]{:T(128)}) while((s32[]{:T(128)}, f32[9,96,1024]{2,1,0:T(8,128)}, bf16[9,96,1024]{2,1,0:T(8,128)(2,1)}, f32[9]{0:T(128)}, ...), condition=%wide.region_3.4_spmd.clone, body=%wide.region_0.3_spmd.clone.sunk | while | flops 229648384 | bytes 11766025 | solution.py:69
  0.5 1.3 convolution_bitcast_fusion.4
  1.8 1.3 convolution_bitcast_fusion.5
  3.7 1.1 convert_reduce_fusion.2
  5.5 3.0 %fusion.91 = f32[9,96,1024]{2,1,0:T(8,128)} fusion(f32[9,96,1024]{2,1,0:T(8,128)} %get-tuple-element.142, s32[]{:T(128)} %get-tuple-element.141, f32[1024,96]{0,1:T(8,128)S(1)} %fusion.90, f32[384,1024]{1,0:T(8,128)S(1)} %convolution_bitcast_fusion.4, f32[384,1024]{1,0:T(8,128)S(1)} %convolution_bitcast_fusion.5, f32[1024]{0:T(1024)S(1)} %get-tuple-element.132, ...), kind=kOutput, calls=%fused_computation.11.clone.1 | convolution fusion | flops 39426048 | bytes 4137984 | tf_op jit(solution)/shard_map/while/body/eval_jaxpr/dot_general | solution.py:60
  8.5 1.3 convolution_bitcast_fusion.4
  9.8 1.3 convolution_bitcast_fusion.5
  13.5 3.0 %fusion.91 = f32[9,96,1024]{2,1,0:T(8,128)} fusion(f32[9,96,1024]{2,1,0:T(8,128)} %get-tuple-element.142, s32[]{:T(128)} %get-tuple-element.141, f32[1024,96]{0,1:T(8,128)S(1)} %fusion.90, f32[384,1024]{1,0:T(8,128)S(1)} %convolution_bitcast_fusion.4, f32[384,1024]{1,0:T(8,128)S(1)} %convolution_bitcast_fusion.5, f32[1024]{0:T(1024)S(1)} %get-tuple-element.132, ...), kind=kOutput, calls=%fused_computation.11.clone.1 | convolution fusion | flops 39426048 | bytes 4137984 | tf_op jit(solution)/shard_map/while/body/eval_jaxpr/dot_general | solution.py:60
  16.5 1.3 convolution_bitcast_fusion.4
  17.8 1.3 convolution_bitcast_fusion.5
  19.7 1.1 convert_reduce_fusion.2
  21.5 3.0 %fusion.91 = f32[9,96,1024]{2,1,0:T(8,128)} fusion(f32[9,96,1024]{2,1,0:T(8,128)} %get-tuple-element.142, s32[]{:T(128)} %get-tuple-element.141, f32[1024,96]{0,1:T(8,128)S(1)} %fusion.90, f32[384,1024]{1,0:T(8,128)S(1)} %convolution_bitcast_fusion.4, f32[384,1024]{1,0:T(8,128)S(1)} %convolution_bitcast_fusion.5, f32[1024]{0:T(1024)S(1)} %get-tuple-element.132, ...), kind=kOutput, calls=%fused_computation.11.clone.1 | convolution fusion | flops 39426048 | bytes 4137984 | tf_op jit(solution)/shard_map/while/body/eval_jaxpr/dot_general | solution.py:60
  24.5 1.3 convolution_bitcast_fusion.4
  25.8 1.3 convolution_bitcast_fusion.5
  27.8 1.1 convert_reduce_fusion.2
  29.5 3.0 %fusion.91 = f32[9,96,1024]{2,1,0:T(8,128)} fusion(f32[9,96,1024]{2,1,0:T(8,128)} %get-tuple-element.142, s32[]{:T(128)} %get-tuple-element.141, f32[1024,96]{0,1:T(8,128)S(1)} %fusion.90, f32[384,1024]{1,0:T(8,128)S(1)} %convolution_bitcast_fusion.4, f32[384,1024]{1,0:T(8,128)S(1)} %convolution_bitcast_fusion.5, f32[1024]{0:T(1024)S(1)} %get-tuple-element.132, ...), kind=kOutput, calls=%fused_computation.11.clone.1 | convolution fusion | flops 39426048 | bytes 4137984 | tf_op jit(solution)/shard_map/while/body/eval_jaxpr/dot_general | solution.py:60
  32.6 1.3 convolution_bitcast_fusion.4
  33.9 1.3 convolution_bitcast_fusion.5
  35.8 1.1 convert_reduce_fusion.2
  37.6 3.0 %fusion.91 = f32[9,96,1024]{2,1,0:T(8,128)} fusion(f32[9,96,1024]{2,1,0:T(8,128)} %get-tuple-element.142, s32[]{:T(128)} %get-tuple-element.141, f32[1024,96]{0,1:T(8,128)S(1)} %fusion.90, f32[384,1024]{1,0:T(8,128)S(1)} %convolution_bitcast_fusion.4, f32[384,1024]{1,0:T(8,128)S(1)} %convolution_bitcast_fusion.5, f32[1024]{0:T(1024)S(1)} %get-tuple-element.132, ...), kind=kOutput, calls=%fused_computation.11.clone.1 | convolution fusion | flops 39426048 | bytes 4137984 | tf_op jit(solution)/shard_map/while/body/eval_jaxpr/dot_general | solution.py:60
  40.6 1.3 convolution_bitcast_fusion.4
  41.9 1.3 convolution_bitcast_fusion.5
  45.6 3.0 %fusion.91 = f32[9,96,1024]{2,1,0:T(8,128)} fusion(f32[9,96,1024]{2,1,0:T(8,128)} %get-tuple-element.142, s32[]{:T(128)} %get-tuple-element.141, f32[1024,96]{0,1:T(8,128)S(1)} %fusion.90, f32[384,1024]{1,0:T(8,128)S(1)} %convolution_bitcast_fusion.4, f32[384,1024]{1,0:T(8,128)S(1)} %convolution_bitcast_fusion.5, f32[1024]{0:T(1024)S(1)} %get-tuple-element.132, ...), kind=kOutput, calls=%fused_computation.11.clone.1 | convolution fusion | flops 39426048 | bytes 4137984 | tf_op jit(solution)/shard_map/while/body/eval_jaxpr/dot_general | solution.py:60
  48.6 1.3 convolution_bitcast_fusion.4
  49.9 1.3 convolution_bitcast_fusion.5
  51.8 1.1 convert_reduce_fusion.2
  53.6 3.0 %fusion.91 = f32[9,96,1024]{2,1,0:T(8,128)} fusion(f32[9,96,1024]{2,1,0:T(8,128)} %get-tuple-element.142, s32[]{:T(128)} %get-tuple-element.141, f32[1024,96]{0,1:T(8,128)S(1)} %fusion.90, f32[384,1024]{1,0:T(8,128)S(1)} %convolution_bitcast_fusion.4, f32[384,1024]{1,0:T(8,128)S(1)} %convolution_bitcast_fusion.5, f32[1024]{0:T(1024)S(1)} %get-tuple-element.132, ...), kind=kOutput, calls=%fused_computation.11.clone.1 | convolution fusion | flops 39426048 | bytes 4137984 | tf_op jit(solution)/shard_map/while/body/eval_jaxpr/dot_general | solution.py:60
  56.6 1.3 convolution_bitcast_fusion.4
  57.9 1.3 convolution_bitcast_fusion.5
  61.6 3.0 %fusion.91 = f32[9,96,1024]{2,1,0:T(8,128)} fusion(f32[9,96,1024]{2,1,0:T(8,128)} %get-tuple-element.142, s32[]{:T(128)} %get-tuple-element.141, f32[1024,96]{0,1:T(8,128)S(1)} %fusion.90, f32[384,1024]{1,0:T(8,128)S(1)} %convolution_bitcast_fusion.4, f32[384,1024]{1,0:T(8,128)S(1)} %convolution_bitcast_fusion.5, f32[1024]{0:T(1024)S(1)} %get-tuple-element.132, ...), kind=kOutput, calls=%fused_computation.11.clone.1 | convolution fusion | flops 39426048 | bytes 4137984 | tf_op jit(solution)/shard_map/while/body/eval_jaxpr/dot_general | solution.py:60
  64.7 1.3 convolution_bitcast_fusion.4
  65.9 1.3 convolution_bitcast_fusion.5
  67.9 1.1 convert_reduce_fusion.2
  69.7 3.0 %fusion.91 = f32[9,96,1024]{2,1,0:T(8,128)} fusion(f32[9,96,1024]{2,1,0:T(8,128)} %get-tuple-element.142, s32[]{:T(128)} %get-tuple-element.141, f32[1024,96]{0,1:T(8,128)S(1)} %fusion.90, f32[384,1024]{1,0:T(8,128)S(1)} %convolution_bitcast_fusion.4, f32[384,1024]{1,0:T(8,128)S(1)} %convolution_bitcast_fusion.5, f32[1024]{0:T(1024)S(1)} %get-tuple-element.132, ...), kind=kOutput, calls=%fused_computation.11.clone.1 | convolution fusion | flops 39426048 | bytes 4137984 | tf_op jit(solution)/shard_map/while/body/eval_jaxpr/dot_general | solution.py:60
  72.7 2.8 %copy.25 = f32[108,8,8,128]{3,2,1,0:T(8,128)S(1)} copy(f32[108,8,8,128]{3,1,2,0:T(8,128)} %bitcast.30) | data formatting | bytes 7077888
  76.2 8.0 %collective-permute-start.1 = (f32[9,96,2,128]{3,2,1,0:T(2,128)S(1)}, f32[9,96,2,128]{3,2,1,0:T(2,128)S(1)}, u32[]{:S(2)}, u32[]{:S(2)}) collective-permute-start(f32[9,96,2,128]{3,2,1,0:T(2,128)S(1)} %get-tuple-element.87), channel_id=1, source_target_pairs={{1,0},{2,1},{3,2},{4,3},{5,4},{6,5},{7,6},{8,7},{9,8},{10,9},{11,1... | collective-permute-start | bytes 2654216 | tf_op jit(solution)/shard_map/ppermute | solution.py:21
  84.3 1.9 %collective-permute-start = (f32[9,96,2,128]{3,2,1,0:T(2,128)S(1)}, f32[9,96,2,128]{3,2,1,0:T(2,128)S(1)}, u32[]{:S(2)}, u32[]{:S(2)}) collective-permute-start(f32[9,96,2,128]{3,2,1,0:T(2,128)S(1)} %get-tuple-element.88), channel_id=1, source_target_pairs={{0,1},{1,2},{2,3},{3,4},{4,5},{5,6},{6,7},{7,8},{8,9},{9,10},{10,1... | collective-permute-start | bytes 2654216 | tf_op jit(solution)/shard_map/ppermute | solution.py:19
  87.3 7.5 %collective-permute-done.1 = f32[9,96,2,128]{3,2,1,0:T(2,128)S(1)} collective-permute-done((f32[9,96,2,128]{3,2,1,0:T(2,128)S(1)}, f32[9,96,2,128]{3,2,1,0:T(2,128)S(1)}, u32[]{:S(2)}, u32[]{:S(2)}) %collective-permute-start.1) | collective-permute-done | bytes 884768 | tf_op jit(solution)/shard_map/ppermute | solution.py:21
  95.2 7.1 %collective-permute-done = f32[9,96,2,128]{3,2,1,0:T(2,128)S(1)} collective-permute-done((f32[9,96,2,128]{3,2,1,0:T(2,128)S(1)}, f32[9,96,2,128]{3,2,1,0:T(2,128)S(1)}, u32[]{:S(2)}, u32[]{:S(2)}) %collective-permute-start) | collective-permute-done | bytes 884768 | tf_op jit(solution)/shard_map/ppermute | solution.py:19
  102.2 6.1 %fusion.49 = bf16[9,96,8,128]{3,2,1,0:T(8,128)(2,1)S(1)} fusion(f32[9,96,2,128]{3,2,1,0:T(2,128)S(1)} %collective-permute-done, f32[9,96,8,128]{3,2,1,0:T(8,128)S(1)} %bitcast.117, f32[9,96,10,128]{3,2,1,0:T(8,128)S(1)} %constant_dynamic-update-slice_fusion, f32[9,8,128]{2,1,0:T(8,128)S(1)} %bitcast.122, f32[9,8,128]{2,1,0:T(8,128)S(1)} %bitcast.120, ...), kind=kLoop, calls=%fused_computation.63 | loop fusion | flops 23003136 | bytes 13391872 | tf_op jit(solution)/shard_map/convert_element_type | solution.py:95
  115.1 5.9 %all-to-all-start = ((bf16[8,9,96,128]{3,2,1,0:T(8,128)(2,1)}), bf16[8,9,96,128]{3,2,1,0:T(8,128)(2,1)S(1)}, u32[]{:S(2)}, u32[]{:S(2)}) async-start(bf16[8,9,96,128]{3,2,1,0:T(8,128)(2,1)} %fusion.60), calls=%async_computation | async-start | bytes 3538944 | tf_op jit(solution)/shard_map/all_to_all | solution.py:102
  121.1 1.8 %and_select_fusion = bf16[72,72,128]{2,1,0:T(8,128)(2,1)S(1)} fusion(bf16[72,72,128]{2,1,0:T(8,128)(2,1)} %param.14, pred[72,128]{1,0:T(8,128)(4,1)S(1)} %iota_compare_fusion), kind=kLoop, calls=%fused_computation.78 | loop fusion | flops 1327104 | bytes 2663424 | tf_op jit(solution)/shard_map/jit(_where)/select_n | solution.py:99
  122.9 2.7 %copy.22 = bf16[72,72,128]{0,1,2:T(8,128)(2,1)} copy(bf16[72,72,128]{2,1,0:T(8,128)(2,1)S(1)} %and_select_fusion) | data formatting | bytes 2654208 | tf_op jit(solution)/shard_map/jit(_where)/select_n | solution.py:99
  125.6 9.3 %all-to-all-done = bf16[8,9,96,128]{3,2,1,0:T(8,128)(2,1)S(1)} async-done(((bf16[8,9,96,128]{3,2,1,0:T(8,128)(2,1)}), bf16[8,9,96,128]{3,2,1,0:T(8,128)(2,1)S(1)}, u32[]{:S(2)}, u32[]{:S(2)}) %all-to-all-start) | async-done | bytes 1769504 | tf_op jit(solution)/shard_map/all_to_all | solution.py:102
  134.9 2.7 %copy.23 = bf16[72,96,128]{1,0,2:T(8,128)(2,1)} copy(bf16[72,96,128]{2,1,0:T(8,128)(2,1)S(1)} %bitcast.118) | data formatting | bytes 3538944 | tf_op jit(solution)/shard_map/reshape | solution.py:103
  137.7 5.9 %fusion.75 = f32[128,72,96]{2,1,0:T(8,128)} fusion(bf16[72,72,128]{0,1,2:T(8,128)(2,1)} %copy.22, bf16[72,96,128]{1,0,2:T(8,128)(2,1)} %copy.23), kind=kOutput, calls=%fused_computation.121 | convolution fusion | flops 127401984 | bytes 6635520 | tf_op jit(solution)/shard_map/obc,oic->ibc/dot_general | solution.py:104
  143.6 5.7 %copy.24 = f32[128,72,96]{0,2,1:T(8,128)} copy(f32[128,72,96]{2,1,0:T(8,128)} %fusion.75) | data formatting | bytes 7077888 | tf_op jit(solution)/shard_map/obc,oic->ibc/dot_general | solution.py:104
  149.2 4.3 %bitcast_add_fusion = f32[72,96,128]{2,1,0:T(8,128)} fusion(f32[128,72,96]{0,2,1:T(8,128)} %copy.24, bf16[8,9,96,128]{3,2,1,0:T(8,128)(2,1)S(1)} %all-to-all-done), kind=kLoop, calls=%fused_computation.77 | loop fusion | flops 1769472 | bytes 8847360 | tf_op jit(solution)/shard_map/add | solution.py:105
  (64 shorter events, 24.4 us)
Async XLA Ops:
  1.8 3.0 %copy-start.3 = (f32[9]{0:T(128)S(1)}, f32[9]{0:T(128)}, u32[]{:S(2)}) copy-start(f32[9]{0:T(128)} %get-tuple-element.151) | copy-start | bytes 112 | tf_op jit(solution)/shard_map/while
  9.8 3.0 %copy-start.3 = (f32[9]{0:T(128)S(1)}, f32[9]{0:T(128)}, u32[]{:S(2)}) copy-start(f32[9]{0:T(128)} %get-tuple-element.151) | copy-start | bytes 112 | tf_op jit(solution)/shard_map/while
  17.8 3.0 %copy-start.3 = (f32[9]{0:T(128)S(1)}, f32[9]{0:T(128)}, u32[]{:S(2)}) copy-start(f32[9]{0:T(128)} %get-tuple-element.151) | copy-start | bytes 112 | tf_op jit(solution)/shard_map/while
  25.8 3.0 %copy-start.3 = (f32[9]{0:T(128)S(1)}, f32[9]{0:T(128)}, u32[]{:S(2)}) copy-start(f32[9]{0:T(128)} %get-tuple-element.151) | copy-start | bytes 112 | tf_op jit(solution)/shard_map/while
  33.8 3.0 %copy-start.3 = (f32[9]{0:T(128)S(1)}, f32[9]{0:T(128)}, u32[]{:S(2)}) copy-start(f32[9]{0:T(128)} %get-tuple-element.151) | copy-start | bytes 112 | tf_op jit(solution)/shard_map/while
  41.9 3.0 %copy-start.3 = (f32[9]{0:T(128)S(1)}, f32[9]{0:T(128)}, u32[]{:S(2)}) copy-start(f32[9]{0:T(128)} %get-tuple-element.151) | copy-start | bytes 112 | tf_op jit(solution)/shard_map/while
  49.9 3.0 %copy-start.3 = (f32[9]{0:T(128)S(1)}, f32[9]{0:T(128)}, u32[]{:S(2)}) copy-start(f32[9]{0:T(128)} %get-tuple-element.151) | copy-start | bytes 112 | tf_op jit(solution)/shard_map/while
  57.9 3.0 %copy-start.3 = (f32[9]{0:T(128)S(1)}, f32[9]{0:T(128)}, u32[]{:S(2)}) copy-start(f32[9]{0:T(128)} %get-tuple-element.151) | copy-start | bytes 112 | tf_op jit(solution)/shard_map/while
  65.9 3.0 %copy-start.3 = (f32[9]{0:T(128)S(1)}, f32[9]{0:T(128)}, u32[]{:S(2)}) copy-start(f32[9]{0:T(128)} %get-tuple-element.151) | copy-start | bytes 112 | tf_op jit(solution)/shard_map/while
  75.5 10.7 %copy-start.1 = (s32[2,1024]{1,0:T(2,128)S(1)}, s32[2,1024]{1,0:T(2,128)}, u32[]{:S(2)}) copy-start(s32[2,1024]{1,0:T(2,128)} %param.13) | copy-start | bytes 24580
  76.2 18.6 %collective-permute-start.1 = (f32[9,96,2,128]{3,2,1,0:T(2,128)S(1)}, f32[9,96,2,128]{3,2,1,0:T(2,128)S(1)}, u32[]{:S(2)}, u32[]{:S(2)}) collective-permute-start(f32[9,96,2,128]{3,2,1,0:T(2,128)S(1)} %get-tuple-element.87), channel_id=1, source_target_pairs={{1,0},{2,1},{3,2},{4,3},{5,4},{6,5},{7,6},{8,7},{9,8},{10,9},{11,1... | collective-permute-start | bytes 2654216 | tf_op jit(solution)/shard_map/ppermute | solution.py:21
  84.3 18.0 %collective-permute-start = (f32[9,96,2,128]{3,2,1,0:T(2,128)S(1)}, f32[9,96,2,128]{3,2,1,0:T(2,128)S(1)}, u32[]{:S(2)}, u32[]{:S(2)}) collective-permute-start(f32[9,96,2,128]{3,2,1,0:T(2,128)S(1)} %get-tuple-element.88), channel_id=1, source_target_pairs={{0,1},{1,2},{2,3},{3,4},{4,5},{5,6},{6,7},{7,8},{8,9},{9,10},{10,1... | collective-permute-start | bytes 2654216 | tf_op jit(solution)/shard_map/ppermute | solution.py:19
  86.3 0.9 copy-start
  112.9 8.2 %copy-start.2 = (s32[128]{0:T(128)S(1)}, s32[128]{0:T(128)}, u32[]{:S(2)}) copy-start(s32[128]{0:T(128)} %param.15) | copy-start | bytes 1540
  115.1 19.8 %all-to-all-start = ((bf16[8,9,96,128]{3,2,1,0:T(8,128)(2,1)}), bf16[8,9,96,128]{3,2,1,0:T(8,128)(2,1)S(1)}, u32[]{:S(2)}, u32[]{:S(2)}) async-start(bf16[8,9,96,128]{3,2,1,0:T(8,128)(2,1)} %fusion.60), calls=%async_computation | async-start | bytes 3538944 | tf_op jit(solution)/shard_map/all_to_all | solution.py:102
